TPU v7x, 512 devices: a whole 4x4x16 slice. The times are simulated.
512 devices in a mesh: mp: 8 (over y, core), tx: 4 (over z_hi), ty: 16 (over x, z_lo).
Axes of the slice: x: 4, y: 4, z: 16 (z_hi: 4, z_lo: 4; z = z_hi * 4 + z_lo), core: 2. Of those that a mesh axis runs over, the one named last changes fastest.
Arguments:
- models: float32 [8, 16, 256, 512], P('mp', None, 'ty', 'tx'), may hold values from -6 to 6
- direction: float32 [8, 16, 256, 512], P('mp', None, 'ty', 'tx'), may hold values from -6 to 6
- coupling: float32 [8], replicated, may hold values from 0.1 to 0.4
- tv_weight: float32 [8], replicated, may hold values from 0.5 to 2
Outputs:
- gradient: float32 [8, 16, 256, 512], P('mp', None, 'ty', 'tx')
- hessian_vector: float32 [8, 16, 256, 512], P('mp', None, 'ty', 'tx')
All inputs are finite; a program needn't handle non-finite values.
Results may differ from a plain program's by a relative error of at most 0.0001.
Values sent between devices are 32-bit elements; how exact they have to be, the bound alone decides.
A program may use at most 64 MiB of HBM per device.

v0:
```python
import jax
import jax.numpy as jnp
from jax import lax
from jax.sharding import PartitionSpec as P

EPS_SQ = 0.25
SYM_PAIRS = ((0, 0), (1, 1), (2, 2), (0, 1), (0, 2), (1, 2))


def passed_along(array, axis, by):
    size = lax.axis_size(axis)
    pairs = [(i, i + by) for i in range(size) if 0 <= i + by < size]
    return lax.ppermute(array, axis, pairs)


def edge_masks(width_y, width_x):
    end_x = lax.axis_index("tx") == lax.axis_size("tx") - 1
    end_y = lax.axis_index("ty") == lax.axis_size("ty") - 1
    col_x = lax.broadcasted_iota(jnp.int32, (1, 1, width_x), 2)
    row_y = lax.broadcasted_iota(jnp.int32, (1, width_y, 1), 1)
    return ((col_x == width_x - 1) & end_x, (row_y == width_y - 1) & end_y)


def fields(tile, rim_x, rim_y):
    last_x, last_y = edge_masks(tile.shape[3], tile.shape[4])
    dx = jnp.concatenate([tile[..., 1:], rim_x], -1) - tile
    dx = jnp.where(last_x, 0.0, dx)
    dy = jnp.concatenate([tile[..., 1:, :], rim_y], -2) - tile
    dy = jnp.where(last_y, 0.0, dy)
    dz = jnp.concatenate(
        [tile[..., 1:, :, :] - tile[..., :-1, :, :], jnp.zeros_like(tile[..., :1, :, :])], -3
    )
    grads = jnp.stack([dx[:, 0], dy[:, 0], dz[:, 0]], 1)
    dirs = jnp.stack([dx[:, 1], dy[:, 1], dz[:, 1]], 1)
    return (grads, dirs)


def moments(grads, dirs, weights):
    wts = weights[:, None, None, None]
    rows = [jnp.sum(wts * grads[:, i] * grads[:, j], 0) for i, j in SYM_PAIRS]
    for i in range(3):
        for j in range(3):
            rows.append(jnp.sum(wts * dirs[:, i] * grads[:, j], 0))
    return jnp.stack(rows, 0)


def couple(moms, grad_own, dir_own):
    trace_m = moms[0] + moms[1] + moms[2]
    mat = [[moms[0], moms[3], moms[4]], [moms[3], moms[1], moms[5]], [moms[4], moms[5], moms[2]]]
    nat = [[moms[6 + 3 * i + j] for j in range(3)] for i in range(3)]
    trace_n = nat[0][0] + nat[1][1] + nat[2][2]
    g_parts = [grad_own[..., i, :, :, :] for i in range(3)]
    e_parts = [dir_own[..., i, :, :, :] for i in range(3)]
    cross_q = []
    cross_p = []
    for i in range(3):
        mg = mat[i][0] * g_parts[0] + mat[i][1] * g_parts[1] + mat[i][2] * g_parts[2]
        me = mat[i][0] * e_parts[0] + mat[i][1] * e_parts[1] + mat[i][2] * e_parts[2]
        ng = nat[i][0] * g_parts[0] + nat[i][1] * g_parts[1] + nat[i][2] * g_parts[2]
        cross_q.append(trace_m * g_parts[i] - mg)
        cross_p.append(trace_m * e_parts[i] - me + trace_n * g_parts[i] - ng)
    return (jnp.stack(cross_q, axis=-4), jnp.stack(cross_p, axis=-4))


def model_split(own, rim_x, rim_y, alpha, beta, own_weights):
    grads, dirs = fields(own, rim_x, rim_y)
    moms = lax.psum(moments(grads, dirs, own_weights), "mp")
    grad_own = grads[0]
    dir_own = dirs[0]
    cross_q, cross_p = couple(moms, grad_own, dir_own)
    size = jnp.sqrt(jnp.sum(grad_own * grad_own, 0) + EPS_SQ)[None]
    flux = jnp.stack(
        [beta * grad_own / size + alpha * cross_q, beta * dir_own / size + alpha * cross_p], 0
    )
    last_x, last_y = edge_masks(flux.shape[3], flux.shape[4])
    flux_x = jnp.where(last_x, 0.0, flux[:, 0])
    flux_y = jnp.where(last_y, 0.0, flux[:, 1])
    flux_z = flux[:, 2]
    flux_z = jnp.concatenate([flux_z[..., :-1, :, :], jnp.zeros_like(flux_z[..., :1, :, :])], -3)
    prev_x = passed_along(flux_x[..., -1:], "tx", 1)
    prev_y = passed_along(flux_y[..., -1:, :], "ty", 1)
    result = jnp.concatenate([prev_x, flux_x[..., :-1]], -1) - flux_x
    result = result + jnp.concatenate([prev_y, flux_y[..., :-1, :]], -2) - flux_y
    result = (
        result
        + jnp.concatenate([jnp.zeros_like(flux_z[..., :1, :, :]), flux_z[..., :-1, :, :]], -3)
        - flux_z
    )
    return (result[0][None], result[1][None])


def shards(models, direction, coupling, tv_weight):
    member = lax.axis_index("mp")
    own_weights = lax.dynamic_slice_in_dim(coupling, member, 1)
    alpha = own_weights[0]
    beta = lax.dynamic_slice_in_dim(tv_weight, member, 1)[0]
    own = jnp.stack([models, direction], 1)
    rim_x = passed_along(own[..., :1], "tx", -1)
    rim_y = passed_along(own[..., :1, :], "ty", -1)
    return model_split(own, rim_x, rim_y, alpha, beta, own_weights)


def solution(mesh):
    placed = (P("mp", None, "ty", "tx"), P("mp", None, "ty", "tx"), P(), P())
    return jax.shard_map(
        shards,
        mesh=mesh,
        in_specs=placed,
        out_specs=(P("mp", None, "ty", "tx"), P("mp", None, "ty", "tx")),
        check_vma=False,
    )
```

profile of v0, /device:TPU:189, one launch (start us, length us, event | category | flops | bytes accessed | tf_op | source)
XLA Modules:
  0.0 180.9 jit_solution(12622415857025574119)
XLA Ops:
  7.2 0.0 copy-start.1
  7.2 0.0 copy-start.2
  7.2 0.0 copy-start.5
  7.2 0.0 all-reduce.4.cloned.1.call-start
  7.2 0.9 fusion.75
  8.2 1.9 %collective-permute-start.1 = (f32[1,2,16,1,128]{4,3,2,1,0:T(1,128)S(1)}, f32[1,2,16,1,128]{4,3,2,1,0:T(1,128)S(1)}, u32[]{:S(2)}, u32[]{:S(2)}) collective-permute-start(f32[1,2,16,1,128]{4,3,2,1,0:T(1,128)S(1)} %fusion.75), channel_id=1, source_target_pairs={{1,0},{2,1},{3,2},{4,3},{5,4},{6,5},{7,6},{8,7},{9,8},{10,9},{11,1... | collective-permute-start | bytes 49160 | tf_op jit(solution)/shard_map/ppermute | solution.py:13
  10.1 1.0 fusion.6
  11.1 1.9 %collective-permute-start = (f32[1,2,16,16,1]{4,3,2,1,0:T(8,128)S(1)}, f32[1,2,16,16,1]{4,3,2,1,0:T(8,128)S(1)}, u32[]{:S(2)}, u32[]{:S(2)}) collective-permute-start(f32[1,2,16,16,1]{4,3,2,1,0:T(8,128)S(1)} %fusion.6), channel_id=1, source_target_pairs={{16,0},{32,16},{48,32},{17,1},{33,17},{49,33},{18,2},{34,18},{50,3... | collective-permute-start | bytes 6152 | tf_op jit(solution)/shard_map/ppermute | solution.py:13
  13.0 1.0 fusion.7
  14.0 1.1 fusion.5
  15.1 1.1 fusion.22
  16.3 0.0 copy-done.5
  16.3 0.6 dynamic_slice.7
  16.9 20.5 %collective-permute-done = f32[1,2,16,16,1]{4,3,2,1,0:T(8,128)S(1)} collective-permute-done((f32[1,2,16,16,1]{4,3,2,1,0:T(8,128)S(1)}, f32[1,2,16,16,1]{4,3,2,1,0:T(8,128)S(1)}, u32[]{:S(2)}, u32[]{:S(2)}) %collective-permute-start) | collective-permute-done | bytes 2080 | tf_op jit(solution)/shard_map/ppermute | solution.py:13
  37.4 0.0 collective-permute-done.1
  37.4 0.0 copy-done.1
  37.4 0.0 copy-done.2
  37.4 0.2 fusion.16
  37.5 0.7 fusion.24
  38.2 0.7 fusion.27
  38.9 0.7 fusion.29
  39.5 0.7 fusion.25
  40.2 0.7 fusion.26
  40.9 0.7 fusion.28
  41.6 0.7 fusion.72
  42.2 0.7 fusion.66
  42.9 0.7 fusion.54
  43.6 0.7 fusion.73
  44.2 0.7 fusion.67
  44.9 0.0 copy-start.6
  44.9 0.7 fusion.55
  45.6 0.7 fusion.74
  46.3 0.7 fusion.68
  46.9 0.7 fusion.56
  47.6 0.0 copy-start.3
  47.6 1.3 copy-done.3
  48.9 0.0 all-reduce.4.cloned.1.call-update
  48.9 0.0 copy-done.6
  48.9 0.6 dynamic_slice.6
  49.6 87.2 %all-reduce.4.cloned.1.call-done = f32[15,16,16,128]{3,2,1,0:T(8,128)} async-done(((f32[15,16,16,128]{3,2,1,0:T(8,128)}), f32[15,16,16,128]{3,2,1,0:T(8,128)}) %all-reduce.4.cloned.1.call-update) | async-done | bytes 1966096 | tf_op jit(solution)/shard_map/psum | solution.py:67
  136.8 0.0 copy-start
  136.8 1.6 fusion.40
  138.5 0.4 copy-done
  138.9 0.1 fusion.36
  139.0 0.1 fusion.33
  139.1 0.1 fusion.59
  139.2 1.4 fusion.1
  140.6 1.4 fusion.4
  141.9 0.0 copy-start.4
  142.0 0.1 fusion.13
  142.0 0.1 slice.200
  142.2 6.5 %collective-permute-start.2 = (f32[2,16,16,1]{3,2,1,0:T(8,128)S(1)}, f32[2,16,16,1]{3,2,1,0:T(8,128)S(1)}, u32[]{:S(2)}, u32[]{:S(2)}) collective-permute-start(f32[2,16,16,1]{3,2,1,0:T(8,128)S(1)} %slice.200), channel_id=1, source_target_pairs={{0,16},{16,32},{32,48},{1,17},{17,33},{33,49},{2,18},{18,34},{34,5... | collective-permute-start | bytes 6152 | tf_op jit(solution)/shard_map/ppermute | solution.py:13
  148.7 2.3 %collective-permute-start.3 = (f32[2,16,1,128]{3,2,1,0:T(1,128)S(1)}, f32[2,16,1,128]{3,2,1,0:T(1,128)S(1)}, u32[]{:S(2)}, u32[]{:S(2)}) collective-permute-start(f32[2,16,1,128]{3,2,1,0:T(1,128)S(1)} %slice.204), channel_id=1, source_target_pairs={{0,1},{1,2},{2,3},{3,4},{4,5},{5,6},{6,7},{7,8},{8,9},{9,10},{10,1... | collective-permute-start | bytes 49160 | tf_op jit(solution)/shard_map/ppermute | solution.py:13
  151.0 10.5 %collective-permute-done.2 = f32[2,16,16,1]{3,2,1,0:T(8,128)S(1)} collective-permute-done((f32[2,16,16,1]{3,2,1,0:T(8,128)S(1)}, f32[2,16,16,1]{3,2,1,0:T(8,128)S(1)}, u32[]{:S(2)}, u32[]{:S(2)}) %collective-permute-start.2) | collective-permute-done | bytes 2080 | tf_op jit(solution)/shard_map/ppermute | solution.py:13
  161.6 11.6 %collective-permute-done.3 = f32[2,16,1,128]{3,2,1,0:T(1,128)S(1)} collective-permute-done((f32[2,16,1,128]{3,2,1,0:T(1,128)S(1)}, f32[2,16,1,128]{3,2,1,0:T(1,128)S(1)}, u32[]{:S(2)}, u32[]{:S(2)}) %collective-permute-start.3) | collective-permute-done | bytes 16416 | tf_op jit(solution)/shard_map/ppermute | solution.py:13
  173.1 0.0 copy-done.4
  173.1 0.2 fusion.20
  173.3 0.7 fusion.76
  (9 shorter events, 0.2 us)
Async XLA Ops:
  7.2 30.2 %copy-start.1 = (f32[1,16,16,128]{3,2,1,0:T(8,128)S(1)}, f32[1,16,16,128]{3,2,1,0:T(8,128)}, u32[]{:S(2)}) copy-start(f32[1,16,16,128]{3,2,1,0:T(8,128)} %param.4) | copy-start | bytes 393220
  7.2 30.2 %copy-start.2 = (f32[1,16,16,128]{3,2,1,0:T(8,128)S(1)}, f32[1,16,16,128]{3,2,1,0:T(8,128)}, u32[]{:S(2)}) copy-start(f32[1,16,16,128]{3,2,1,0:T(8,128)} %param.5) | copy-start | bytes 393220
  7.2 9.1 %copy-start.5 = (f32[8]{0:T(128)S(1)}, f32[8]{0:T(128)}, u32[]{:S(2)}) copy-start(f32[8]{0:T(128)} %param.6) | copy-start | bytes 100
  7.2 129.6 %all-reduce.4.cloned.1.call-start = ((), (), s32[]{:S(2)}) async-start(), calls=%async_computation | async-start | bytes 3932160 | tf_op jit(solution)/shard_map/psum | solution.py:67
  8.2 29.2 %collective-permute-start.1 = (f32[1,2,16,1,128]{4,3,2,1,0:T(1,128)S(1)}, f32[1,2,16,1,128]{4,3,2,1,0:T(1,128)S(1)}, u32[]{:S(2)}, u32[]{:S(2)}) collective-permute-start(f32[1,2,16,1,128]{4,3,2,1,0:T(1,128)S(1)} %fusion.75), channel_id=1, source_target_pairs={{1,0},{2,1},{3,2},{4,3},{5,4},{6,5},{7,6},{8,7},{9,8},{10,9},{11,1... | collective-permute-start | bytes 49160 | tf_op jit(solution)/shard_map/ppermute | solution.py:13
  11.1 26.3 %collective-permute-start = (f32[1,2,16,16,1]{4,3,2,1,0:T(8,128)S(1)}, f32[1,2,16,16,1]{4,3,2,1,0:T(8,128)S(1)}, u32[]{:S(2)}, u32[]{:S(2)}) collective-permute-start(f32[1,2,16,16,1]{4,3,2,1,0:T(8,128)S(1)} %fusion.6), channel_id=1, source_target_pairs={{16,0},{32,16},{48,32},{17,1},{33,17},{49,33},{18,2},{34,18},{50,3... | collective-permute-start | bytes 6152 | tf_op jit(solution)/shard_map/ppermute | solution.py:13
  44.9 4.0 %copy-start.6 = (f32[8]{0:T(128)S(1)}, f32[8]{0:T(128)}, u32[]{:S(2)}) copy-start(f32[8]{0:T(128)} %param.7) | copy-start | bytes 100
  47.6 1.3 copy-start.3
  136.8 2.0 %copy-start = (f32[15,16,16,128]{3,2,1,0:T(8,128)S(1)}, f32[15,16,16,128]{3,2,1,0:T(8,128)}, u32[]{:S(2)}) copy-start(f32[15,16,16,128]{3,2,1,0:T(8,128)} %all-reduce.4.cloned.1.call-done) | copy-start | bytes 5898244
  141.9 31.2 %copy-start.4 = (pred[16]{0:T(512)(128)(4,1)S(1)}, pred[16]{0:T(512)(128)(4,1)}, u32[]{:S(2)}) copy-start(pred[16]{0:T(512)(128)(4,1)} %constant.33.clone.1) | copy-start | bytes 52
  142.2 19.4 %collective-permute-start.2 = (f32[2,16,16,1]{3,2,1,0:T(8,128)S(1)}, f32[2,16,16,1]{3,2,1,0:T(8,128)S(1)}, u32[]{:S(2)}, u32[]{:S(2)}) collective-permute-start(f32[2,16,16,1]{3,2,1,0:T(8,128)S(1)} %slice.200), channel_id=1, source_target_pairs={{0,16},{16,32},{32,48},{1,17},{17,33},{33,49},{2,18},{18,34},{34,5... | collective-permute-start | bytes 6152 | tf_op jit(solution)/shard_map/ppermute | solution.py:13
  148.7 24.5 %collective-permute-start.3 = (f32[2,16,1,128]{3,2,1,0:T(1,128)S(1)}, f32[2,16,1,128]{3,2,1,0:T(1,128)S(1)}, u32[]{:S(2)}, u32[]{:S(2)}) collective-permute-start(f32[2,16,1,128]{3,2,1,0:T(1,128)S(1)} %slice.204), channel_id=1, source_target_pairs={{0,1},{1,2},{2,3},{3,4},{4,5},{5,6},{6,7},{7,8},{8,9},{9,10},{10,1... | collective-permute-start | bytes 49160 | tf_op jit(solution)/shard_map/ppermute | solution.py:13
Sparse Core Ops, SparseCore 0:
  49.0 87.7 all-reduce.3
where the time goes:
time: 181 us
  waiting for transfers between devices  130 us (72%)
  other arithmetic  20.3 us (11%)
  between operations  14.4 us (8%)
  starting transfers between devices  12.6 us (7%)
  local copies, waits for them, and re-layouts  3.79 us (2%)
    psum x1, waiting for transfers between devices, model_split(): moms = lax.psum(moments(grads, dirs, own_weights), 'mp')  87.2 us
    ppermute x4, waiting for transfers between devices, passed_along(): return lax.ppermute(array, axis, pairs)  42.6 us
    ppermute x4, starting transfers between devices, passed_along(): return lax.ppermute(array, axis, pairs)  12.6 us
    unnamed x14, other arithmetic  9.27 us
    another operation x4, other arithmetic, shards(): own = jnp.stack([models, direction], 1)  4.02 us
  transfers between devices with their start and end apart: 5, of which 4 were waited for; matrix products, arithmetic and copies ran while one was open for 3% of the time, Pallas kernels for 0%

commit v1 on v0

v1 whole, which is shorter than its diff:
```python
import functools

import jax
import jax.numpy as jnp
from jax import lax
from jax.experimental import pallas as pl
from jax.experimental.pallas import tpu as pltpu
from jax.sharding import PartitionSpec as P

EPS_SQ = 0.25
MESH = pl.DeviceIdType.MESH
MODELS = 8
CHIPS = 4
NZ = 16
ROWS = 16
LANES = 128
SLABS = 38
COLS = 36

RING = ("O0", "O1", "B0", "B1", "HO", "HB", "F0", "F1", "FH")
NAMES = (
    ["ty0", "ty1", "tx0", "tx1", "S1", "S0", "SH"]
    + [d + k for d in "+-" for k in RING]
    + ["X" + d + k for d in "+-" for k in RING]
    + ["P%d%d" % (a, b) for a in range(CHIPS) for b in range(2) if a + b > 0]
)
INDEX = {name: i for i, name in enumerate(NAMES)}


def kernel(
    x_hbm, d_hbm, coupling, tv_weight, gout, hout,
    held, tile, moms, own_cols, got_cols, col_flux, in_sem, send_sem, recv_sem,
):
    mp, tx, ty = (lax.axis_index(a) for a in ("mp", "tx", "ty"))
    n_tx, n_ty = lax.axis_size("tx"), lax.axis_size("ty")
    chip, core = mp // 2, mp % 2
    sib = 1 - core

    def at_chip(by):
        return lax.rem(chip + by + CHIPS, CHIPS)

    def peer(by, other):
        return (at_chip(by) * 2 + (sib if other else core), tx, ty)

    left = (mp, lax.rem(tx + n_tx - 1, n_tx), ty)
    right = (mp, lax.rem(tx + 1, n_tx), ty)
    before = (mp, tx, lax.rem(ty + n_ty - 1, n_ty))
    after = (mp, tx, lax.rem(ty + 1, n_ty))
    peers = [(a, b) for a in range(CHIPS) for b in range(2) if a + b > 0]

    loads = [
        pltpu.make_async_copy(x_hbm, tile.at[0], in_sem.at[0]),
        pltpu.make_async_copy(d_hbm, tile.at[1], in_sem.at[1]),
    ]
    for load in loads:
        load.start()
    barrier = pltpu.get_barrier_semaphore()
    everyone = [peer(a, b) for a, b in peers] + [left, right, before, after]
    for device in everyone:
        pl.semaphore_signal(barrier, inc=1, device_id=device, device_id_type=MESH)

    lane = lax.broadcasted_iota(jnp.int32, (NZ, LANES), 1)
    level = lax.broadcasted_iota(jnp.int32, (NZ, LANES), 0)
    inner_z = level < NZ - 1

    started = []

    def copy(name, src, dst, device):
        i = INDEX[name]
        return pltpu.make_async_remote_copy(
            src_ref=src, dst_ref=dst, send_sem=send_sem.at[i], recv_sem=recv_sem.at[i],
            device_id=device, device_id_type=MESH,
        )

    def send(name, src, device, dst=None):
        c = copy(name, src, src if dst is None else dst, device)
        c.start()
        started.append(c)

    def arrived(name, dst):
        copy(name, dst, dst, peer(0, 1)).wait_recv()

    def piece(owner_chip, owner_core, half, kind):
        model = owner_chip * 2 + owner_core
        if kind == "h":
            return held.at[model, pl.ds(2 - 2 * half, 2)]
        if kind == "all":
            return held.at[model, pl.ds(4 + 16 * half, 16)]
        return held.at[model, pl.ds(4 + 16 * half + 8 * kind, 8)]

    def pack_row(cols, q, r):
        v = held[mp, 2 * ((r + 2) % 18) + q]
        low = pltpu.roll(v, (r + 2) % LANES, 1)
        high = pltpu.roll(v, (r + 97) % LANES, 1)
        cols = jnp.where(lane == r + 1, low, cols)
        return jnp.where(lane == r + 97, high, cols)

    for load in loads:
        load.wait()
    for q in range(2):
        cols = jnp.zeros((NZ, LANES), jnp.float32)
        for r in range(ROWS):
            held[mp, 2 * (r + 2) + q] = tile[q, pl.ds(r, NZ, stride=ROWS), :]
        for r in range(ROWS):
            cols = pack_row(cols, q, r)
        own_cols[q] = cols

    pl.semaphore_wait(barrier, len(everyone))

    send("ty0", held.at[mp, pl.ds(4, 2)], before, held.at[mp, pl.ds(0, 2)])
    send("ty1", held.at[mp, pl.ds(34, 2)], after, held.at[mp, pl.ds(2, 2)])
    send("S1", piece(chip, core, sib, "all"), peer(0, 1))
    send("+O0", piece(chip, core, core, 0), peer(1, 0))
    send("-O1", piece(chip, core, core, 1), peer(-1, 0))
    send("+O1", piece(chip, core, core, 1), peer(1, 0))
    send("-O0", piece(chip, core, core, 0), peer(-1, 0))
    send("S0", piece(chip, core, core, "all"), peer(0, 1))
    arrived("S1", piece(chip, sib, core, "all"))
    send("+B0", piece(chip, sib, core, 0), peer(1, 0))
    send("-B1", piece(chip, sib, core, 1), peer(-1, 0))
    send("+B1", piece(chip, sib, core, 1), peer(1, 0))
    send("-B0", piece(chip, sib, core, 0), peer(-1, 0))
    arrived("S0", piece(chip, sib, sib, "all"))

    def differences(f, f_next, keep_y=None):
        dx = pltpu.roll(f, LANES - 1, 1) - f
        dy = f_next - f
        if keep_y is not None:
            dy = dy * keep_y
        dz = jnp.where(inner_z, pltpu.roll(f, NZ - 1, 0) - f, 0.0)
        return dx, dy, dz

    def row_fields(model, i):
        here = 2 * (i + 1)
        then = 2 * jnp.where(i == ROWS, 0, i + 2)
        keep = jnp.where((i == ROWS) & (ty == n_ty - 1), 0.0, 1.0)
        g = differences(held[model, here], held[model, then], keep)
        e = differences(held[model, here + 1], held[model, then + 1], keep)
        return g, e

    def add_moments(acc, g, e, weight):
        w = [weight * v for v in g]
        terms = [w[0] * g[0], w[1] * g[1], w[2] * g[2], w[0] * g[1], w[0] * g[2], w[1] * g[2]]
        terms += [e[i] * w[j] for i in range(3) for j in range(3)]
        return terms if acc is None else [a + t for a, t in zip(acc, terms)]

    def gather_rows(models, first, last, fresh):
        def body(i, carry):
            acc = None if fresh else [moms[i, j] for j in range(15)]
            for model in models:
                g, e = row_fields(model, i)
                acc = add_moments(acc, g, e, coupling[model])
            for j in range(15):
                moms[i, j] = acc[j]
            return carry

        lax.fori_loop(first, last, body, 0)

    pair_own = [chip * 2, chip * 2 + 1]
    pair_prev = [at_chip(-1) * 2, at_chip(-1) * 2 + 1]
    pair_next = [at_chip(1) * 2, at_chip(1) * 2 + 1]
    pair_far = [at_chip(2) * 2, at_chip(2) * 2 + 1]

    gather_rows(pair_own, 1, ROWS, True)

    arrived("ty0", held.at[mp, pl.ds(0, 2)])
    arrived("ty1", held.at[mp, pl.ds(2, 2)])
    send("SH", held.at[mp, pl.ds(0, 4)], peer(0, 1))
    send("+HO", piece(chip, core, core, "h"), peer(1, 0))
    send("-HO", piece(chip, core, core, "h"), peer(-1, 0))
    for q in range(2):
        own_cols[q] = pack_row(pack_row(own_cols[q], q, -1), q, ROWS)
    send("tx0", own_cols, left, got_cols.at[0])
    send("tx1", own_cols, right, got_cols.at[1])

    def relay(d, kind, source, owner_core, half_piece):
        ref = piece(source, owner_core, core, half_piece)
        arrived(d + kind, ref)
        send("X" + d + kind, ref, peer(0, 1))
        return ref

    prev, nxt, far = at_chip(-1), at_chip(1), at_chip(2)
    send("+F0", relay("+", "O0", prev, core, 0), peer(1, 0))
    send("-F0", relay("-", "O1", nxt, core, 1), peer(-1, 0))
    arrived("SH", held.at[chip * 2 + sib, pl.ds(0, 4)])
    send("+HB", piece(chip, sib, core, "h"), peer(1, 0))
    send("-HB", piece(chip, sib, core, "h"), peer(-1, 0))
    relay("+", "O1", prev, core, 1)
    relay("-", "O0", nxt, core, 0)
    send("+F1", relay("+", "B0", prev, sib, 0), peer(1, 0))
    send("-F1", relay("-", "B1", nxt, sib, 1), peer(-1, 0))
    relay("+", "B1", prev, sib, 1)
    relay("-", "B0", nxt, sib, 0)
    send("+FH", relay("+", "HO", prev, core, "h"), peer(1, 0))
    relay("-", "HO", nxt, core, "h")
    relay("+", "HB", prev, sib, "h")
    send("-FH", relay("-", "HB", nxt, sib, "h"), peer(-1, 0))

    arrived("tx0", got_cols.at[0])
    arrived("tx1", got_cols.at[1])
    for q in range(2):
        mine = own_cols[q]
        cols = jnp.where(lane < 64, pltpu.roll(got_cols[1, q], 32, 1), pltpu.roll(got_cols[0, q], 96, 1))
        held[mp, COLS + q] = jnp.where((lane < 32) | (lane >= 96), mine, cols)
    for a, b in peers:
        send("P%d%d" % (a, b), held.at[mp, pl.ds(COLS, 2)], peer(a, b))

    for d, source in (("+", prev), ("-", nxt)):
        for kind, other, half_piece in (
            ("O0", 1, 0), ("O1", 1, 1), ("B0", 0, 0), ("B1", 0, 1), ("HO", 1, "h"), ("HB", 0, "h"),
        ):
            owner = sib if other else core
            arrived("X" + d + kind, piece(source, owner, sib, half_piece))

    gather_rows(pair_own, ROWS, ROWS + 1, True)
    gather_rows(pair_own, 0, 1, True)
    gather_rows(pair_prev + pair_next, 0, ROWS + 1, False)

    relay("+", "F0", far, core, 0)
    relay("-", "F0", far, core, 1)
    relay("+", "F1", far, sib, 0)
    relay("-", "F1", far, sib, 1)
    relay("+", "FH", far, core, "h")
    relay("-", "FH", far, sib, "h")
    arrived("X+F0", piece(far, sib, sib, 0))
    arrived("X-F0", piece(far, sib, sib, 1))
    arrived("X+F1", piece(far, core, sib, 0))
    arrived("X-F1", piece(far, core, sib, 1))
    arrived("X+FH", piece(far, sib, sib, "h"))
    arrived("X-FH", piece(far, core, sib, "h"))

    for a, b in peers:
        owner = at_chip(-a) * 2 + (sib if b else core)
        arrived("P%d%d" % (a, b), held.at[owner, pl.ds(COLS, 2)])

    alpha = coupling[mp]
    ratio = tv_weight[mp] / alpha

    def fluxes(m, g, e):
        size_sq = g[0] * g[0] + g[1] * g[1] + g[2] * g[2] + EPS_SQ
        tv = ratio * lax.rsqrt(size_sq)
        a00, a11, a22 = m[1] + m[2] + tv, m[0] + m[2] + tv, m[0] + m[1] + tv
        b00, b11, b22 = m[10] + m[14], m[6] + m[14], m[6] + m[10]
        q = (
            a00 * g[0] - (m[3] * g[1] + m[4] * g[2]),
            a11 * g[1] - (m[3] * g[0] + m[5] * g[2]),
            a22 * g[2] - (m[4] * g[0] + m[5] * g[1]),
        )
        p = (
            (a00 * e[0] + b00 * g[0]) - ((m[3] * e[1] + m[4] * e[2]) + (m[7] * g[1] + m[8] * g[2])),
            (a11 * e[1] + b11 * g[1]) - ((m[3] * e[0] + m[5] * e[2]) + (m[9] * g[0] + m[11] * g[2])),
            (a22 * e[2] + b22 * g[2]) - ((m[4] * e[0] + m[5] * e[1]) + (m[12] * g[0] + m[13] * g[1])),
        )
        return q, p

    def along_z(fz):
        fz = jnp.where(inner_z, fz, 0.0)
        return jnp.where(level == 0, 0.0, pltpu.roll(fz, 1, 0)) - fz

    no_x = (lane < 32) & (tx == n_tx - 1)
    no_y = ((lane == ROWS) | (lane == ROWS + 32)) & (ty == n_ty - 1)

    def col_fields(model):
        out = []
        for q in range(2):
            v = held[model, COLS + q]
            dx = jnp.where(no_x, 0.0, pltpu.roll(v, 64, 1) - v)
            dy = jnp.where(no_y, 0.0, pltpu.roll(v, LANES - 1, 1) - v)
            dz = jnp.where(inner_z, pltpu.roll(v, NZ - 1, 0) - v, 0.0)
            out.append((dx, dy, dz))
        return out

    def col_body(model, acc):
        g, e = col_fields(model)
        return tuple(add_moments(acc, g, e, coupling[model]))

    zero = jnp.zeros((NZ, LANES), jnp.float32)
    col_moms = lax.fori_loop(0, MODELS, col_body, (zero,) * 15)
    off_x = no_x | ((lane >= 32) & (tx == 0))
    off_y = no_y | ((lane == 0) & (ty == 0))
    ends, starts = [], []
    for f in fluxes(col_moms, *col_fields(mp)):
        fx = jnp.where(off_x, 0.0, f[0])
        fy = jnp.where(off_y, 0.0, f[1])
        ends.append(pltpu.roll(fy, 1, 1) - fy + along_z(f[2]) - fx)
        starts.append(fx)
    for q in range(2):
        col_flux[0, q] = ends[q]
        col_flux[1, q] = starts[q]

    outs = (gout, hout)

    def row_flux(i):
        acc = [moms[i, j] for j in range(15)]
        for model in pair_far:
            g, e = row_fields(model, i)
            acc = add_moments(acc, g, e, coupling[model])
        return fluxes(acc, *row_fields(mp, i))

    first = row_flux(0)
    keep_first = jnp.where(ty == 0, 0.0, 1.0)
    carry = tuple(f[1] * keep_first for f in first)

    def out_body(r, carry):
        both = row_flux(r + 1)
        keep = jnp.where((r == ROWS - 1) & (ty == n_ty - 1), 0.0, 1.0)
        new = []
        for q in range(2):
            fx, fy, fz = both[q]
            fy = fy * keep
            before_x = jnp.where(lane == 0, pltpu.roll(col_flux[1, q], 95 - r, 1), pltpu.roll(fx, 1, 1))
            rest = carry[q] - fy + along_z(fz) - fx
            rest = jnp.where(lane == LANES - 1, pltpu.roll(col_flux[0, q], 126 - r, 1), rest)
            outs[q][pl.ds(r, NZ, stride=ROWS), :] = alpha * (before_x + rest)
            new.append(fy)
        return tuple(new)

    lax.fori_loop(0, ROWS, out_body, carry)

    for c in started:
        c.wait_send()


def shards(models, direction, coupling, tv_weight):
    flat = (NZ * ROWS, LANES)
    n = len(NAMES)
    out = pl.pallas_call(
        kernel,
        name="fused",
        out_shape=[jax.ShapeDtypeStruct(flat, jnp.float32)] * 2,
        in_specs=[pl.BlockSpec(memory_space=pl.ANY)] * 2 + [pl.BlockSpec(memory_space=pltpu.SMEM)] * 2,
        out_specs=[pl.BlockSpec(memory_space=pltpu.VMEM)] * 2,
        scratch_shapes=[
            pltpu.VMEM((MODELS, SLABS, NZ, LANES), jnp.float32),
            pltpu.VMEM((2,) + flat, jnp.float32),
            pltpu.VMEM((ROWS + 1, 15, NZ, LANES), jnp.float32),
            pltpu.VMEM((2, NZ, LANES), jnp.float32),
            pltpu.VMEM((2, 2, NZ, LANES), jnp.float32),
            pltpu.VMEM((2, 2, NZ, LANES), jnp.float32),
            pltpu.SemaphoreType.DMA((2,)),
            pltpu.SemaphoreType.DMA((n,)),
            pltpu.SemaphoreType.DMA((n,)),
        ],
        compiler_params=pltpu.CompilerParams(
            collective_id=1, has_side_effects=True, vmem_limit_bytes=60 * 2**20
        ),
    )(models.reshape(flat), direction.reshape(flat), coupling, tv_weight)
    return tuple(o.reshape(models.shape) for o in out)


def solution(mesh):
    placed = (P("mp", None, "ty", "tx"), P("mp", None, "ty", "tx"), P(), P())
    return jax.shard_map(
        shards,
        mesh=mesh,
        in_specs=placed,
        out_specs=(P("mp", None, "ty", "tx"), P("mp", None, "ty", "tx")),
        check_vma=False,
    )
```

time: 181 us -> 38.6 us (0.21)
  the two profiles are of different devices: /device:TPU:189 before, /device:TPU:1 now
where the time goes in v1:
time: 38.6 us; the launch traced here: 38.5 us
  Pallas kernels  35.6 us (92%)
  local copies, waits for them, and re-layouts  2.26 us (6%)
  between operations  0.65 us (2%)
    pallas_call x1, Pallas kernels, shards(): pl.pallas_call(kernel, name='fused', out_shape=[jax.ShapeDtypeStruct(flat...  35.6 us
    unnamed x4, local copies, waits for them, and re-layouts  2.26 us

profile of v1, /device:TPU:1, one launch (start us, length us, event | category | flops | bytes accessed | tf_op | source)
XLA Modules:
  0.0 38.5 jit_solution(7295612469844097168)
XLA Ops:
  0.6 35.6 %fused.1 = (f32[256,128]{1,0:T(8,128)}, f32[256,128]{1,0:T(8,128)}) custom-call(f32[256,128]{1,0:T(8,128)} %bitcast.4, f32[256,128]{1,0:T(8,128)} %bitcast.5, f32[8]{0:T(128)} %coupling.1, f32[8]{0:T(128)} %tv_weight.1), custom_call_target="tpu_custom_call" | custom-call | tf_op jit(solution)/shard_map/fused/pallas_call | solution.py:327
  36.2 0.0 copy-start
  36.2 1.6 %copy.8 = f32[1,16,16,128]{3,2,1,0:T(8,128)} copy(f32[1,16,16,128]{3,2,1,0:T(8,128)} %bitcast.7) | data formatting | bytes 262144
  37.8 0.0 copy-done
  37.8 0.7 %copy.9 = f32[1,16,16,128]{3,2,1,0:T(8,128)} copy(f32[1,16,16,128]{3,2,1,0:T(8,128)S(1)} %bitcast.6) | data formatting | bytes 262144
Async XLA Ops:
  36.2 1.6 %copy-start = (f32[256,128]{1,0:T(8,128)S(1)}, f32[256,128]{1,0:T(8,128)}, u32[]{:S(2)}) copy-start(f32[256,128]{1,0:T(8,128)} %get-tuple-element.5) | copy-start | bytes 393220

commit v2 on v1

v2 whole, which is shorter than its diff:
```python
import functools

import jax
import jax.numpy as jnp
from jax import lax
from jax.experimental import pallas as pl
from jax.experimental.pallas import tpu as pltpu
from jax.sharding import PartitionSpec as P

EPS_SQ = 0.25
MESH = pl.DeviceIdType.MESH
MODELS = 8
CHIPS = 4
NZ = 16
ROWS = 16
LANES = 128
SLABS = 38
COLS = 36

RING = ("O0", "O1", "B0", "B1", "HO", "HB", "F0", "F1", "FH")
NAMES = (
    ["ty0", "ty1", "tx0", "tx1", "S1", "S0", "SH"]
    + [d + k for d in "+-" for k in RING]
    + ["X" + d + k for d in "+-" for k in RING]
    + ["P%d%d" % (a, b) for a in range(CHIPS) for b in range(2) if a + b > 0]
)
INDEX = {name: i for i, name in enumerate(NAMES)}


def kernel(
    x_hbm, d_hbm, coupling_hbm, tv_hbm, gout, hout,
    held, tile, moms, own_cols, got_cols, col_flux, coupling, tv_weight, in_sem, send_sem, recv_sem, leave,
):
    mp, tx, ty = (lax.axis_index(a) for a in ("mp", "tx", "ty"))
    n_tx, n_ty = lax.axis_size("tx"), lax.axis_size("ty")
    chip, core = mp // 2, mp % 2
    sib = 1 - core

    def at_chip(by):
        return lax.rem(chip + by + CHIPS, CHIPS)

    def peer(by, other):
        return (at_chip(by) * 2 + (sib if other else core), tx, ty)

    left, right = (mp, jnp.maximum(tx - 1, 0), ty), (mp, jnp.minimum(tx + 1, n_tx - 1), ty)
    before, after = (mp, tx, jnp.maximum(ty - 1, 0)), (mp, tx, jnp.minimum(ty + 1, n_ty - 1))
    has_left, has_right, has_before, has_after = tx > 0, tx < n_tx - 1, ty > 0, ty < n_ty - 1
    greets_left, greeted_right = tx == n_tx - 1, tx == n_tx - 2
    gives_leave = has_left & jnp.logical_not(greets_left)
    needs_leave = has_right & jnp.logical_not(greeted_right)
    peers = [(a, b) for a in range(CHIPS) for b in range(2) if a + b > 0]

    barrier = pltpu.get_barrier_semaphore()

    def greet(device):
        pl.semaphore_signal(barrier, inc=1, device_id=device, device_id_type=MESH)

    for wanted, device in ((has_before, before), (has_after, after), (has_right, right), (greets_left, left)):
        pl.when(wanted)(functools.partial(greet, device))
    for a, b in peers:
        greet(peer(a, b))
    loads = [
        pltpu.make_async_copy(src, dst, in_sem.at[i])
        for i, (src, dst) in enumerate(
            ((x_hbm, tile.at[0]), (d_hbm, tile.at[1]), (coupling_hbm, coupling), (tv_hbm, tv_weight))
        )
    ]
    for load in loads:
        load.start()

    lane = lax.broadcasted_iota(jnp.int32, (NZ, LANES), 1)
    level = lax.broadcasted_iota(jnp.int32, (NZ, LANES), 0)
    inner_z = level < NZ - 1
    zero = jnp.zeros((NZ, LANES), jnp.float32)

    started = []

    def copy(name, src, dst, device):
        i = INDEX[name]
        return pltpu.make_async_remote_copy(
            src_ref=src, dst_ref=dst, send_sem=send_sem.at[i], recv_sem=recv_sem.at[i],
            device_id=device, device_id_type=MESH,
        )

    def send(name, src, device, dst=None, wanted=None):
        c = copy(name, src, src if dst is None else dst, device)
        if wanted is None:
            c.start()
        else:
            pl.when(wanted)(c.start)
        started.append((wanted, c))

    def arrived(name, dst, wanted=None):
        wait = copy(name, dst, dst, peer(0, 1)).wait_recv
        if wanted is None:
            wait()
        else:
            pl.when(wanted)(wait)

    def piece(owner_chip, owner_core, half, kind):
        model = owner_chip * 2 + owner_core
        if kind == "h":
            return held.at[model, pl.ds(2 - 2 * half, 2)]
        if kind == "all":
            return held.at[model, pl.ds(4 + 16 * half, 16)]
        return held.at[model, pl.ds(4 + 16 * half + 8 * kind, 8)]

    def pack_row(cols, q, r):
        v = held[mp, 2 * ((r + 2) % 18) + q]
        low = pltpu.roll(v, (r + 2) % LANES, 1)
        high = pltpu.roll(v, (r + 97) % LANES, 1)
        cols = jnp.where(lane == r + 1, low, cols)
        return jnp.where(lane == r + 97, high, cols)

    def blank(ref):
        ref[...] = jnp.zeros(ref.shape, jnp.float32)

    rim_after, rim_before = held.at[mp, pl.ds(0, 2)], held.at[mp, pl.ds(2, 2)]
    for missing, ref in (
        (jnp.logical_not(has_after), rim_after), (jnp.logical_not(has_before), rim_before),
        (jnp.logical_not(has_right), got_cols.at[0]), (jnp.logical_not(has_left), got_cols.at[1]),
    ):
        pl.when(missing)(functools.partial(blank, ref))
    for load in loads:
        load.wait()
    for q in range(2):
        for r in range(ROWS):
            held[mp, 2 * (r + 2) + q] = tile[q, pl.ds(r, NZ, stride=ROWS), :]
    for q in range(2):
        cols = zero
        for r in range(ROWS):
            cols = pack_row(cols, q, r)
        own_cols[q] = cols

    expected = len(peers) + sum(w.astype(jnp.int32) for w in (has_before, has_after, has_left, greeted_right))
    pl.semaphore_wait(barrier, expected)

    send("ty0", held.at[mp, pl.ds(4, 2)], before, rim_after, has_before)
    send("ty1", held.at[mp, pl.ds(34, 2)], after, rim_before, has_after)
    send("S1", piece(chip, core, sib, "all"), peer(0, 1))
    send("+O0", piece(chip, core, core, 0), peer(1, 0))
    send("-O1", piece(chip, core, core, 1), peer(-1, 0))
    send("+O1", piece(chip, core, core, 1), peer(1, 0))
    send("-O0", piece(chip, core, core, 0), peer(-1, 0))
    send("S0", piece(chip, core, core, "all"), peer(0, 1))

    def give_leave():
        pl.semaphore_signal(leave, inc=1, device_id=left, device_id_type=MESH)

    pl.when(gives_leave)(give_leave)
    arrived("S1", piece(chip, sib, core, "all"))
    send("+B0", piece(chip, sib, core, 0), peer(1, 0))
    send("-B1", piece(chip, sib, core, 1), peer(-1, 0))
    send("+B1", piece(chip, sib, core, 1), peer(1, 0))
    send("-B0", piece(chip, sib, core, 0), peer(-1, 0))
    arrived("S0", piece(chip, sib, sib, "all"))

    def differences(f, f_next, keep_y=None):
        dx = pltpu.roll(f, LANES - 1, 1) - f
        dy = f_next - f
        if keep_y is not None:
            dy = dy * keep_y
        dz = jnp.where(inner_z, pltpu.roll(f, NZ - 1, 0) - f, 0.0)
        return dx, dy, dz

    keep_last = jnp.where(has_after, 1.0, 0.0)

    def row_fields(model, i):
        here = 2 * (i + 1)
        last = isinstance(i, int) and i == ROWS
        then = 0 if last else 2 * (i + 2)
        keep = keep_last if last else None
        g = differences(held[model, here], held[model, then], keep)
        e = differences(held[model, here + 1], held[model, then + 1], keep)
        return g, e

    def add_moments(acc, g, e, weight):
        w = [weight * v for v in g]
        terms = [w[0] * g[0], w[1] * g[1], w[2] * g[2], w[0] * g[1], w[0] * g[2], w[1] * g[2]]
        terms += [e[i] * w[j] for i in range(3) for j in range(3)]
        return terms if acc is None else [a + t for a, t in zip(acc, terms)]

    def row_moments(acc, models, i):
        for model in models:
            g, e = row_fields(model, i)
            acc = add_moments(acc, g, e, coupling[model])
        return acc

    def gather_rows(models, fresh):
        def body(i, carry):
            acc = row_moments(None if fresh else [moms[i, j] for j in range(15)], models, i)
            for j in range(15):
                moms[i, j] = acc[j]
            return carry

        lax.fori_loop(1, ROWS, body, 0, unroll=5)

    prev, nxt, far = at_chip(-1), at_chip(1), at_chip(2)
    pair_own, pair_prev, pair_next, pair_far = ([c * 2, c * 2 + 1] for c in (chip, prev, nxt, far))

    def relay(d, kind, source, owner_core, half_piece):
        ref = piece(source, owner_core, core, half_piece)
        arrived(d + kind, ref)
        send("X" + d + kind, ref, peer(0, 1))
        return ref

    gather_rows(pair_own, True)

    send("+F0", relay("+", "O0", prev, core, 0), peer(1, 0))
    send("-F0", relay("-", "O1", nxt, core, 1), peer(-1, 0))
    arrived("ty0", rim_after, has_after)
    arrived("ty1", rim_before, has_before)
    send("SH", held.at[mp, pl.ds(0, 4)], peer(0, 1))
    send("+HO", piece(chip, core, core, "h"), peer(1, 0))
    send("-HO", piece(chip, core, core, "h"), peer(-1, 0))
    for q in range(2):
        own_cols[q] = pack_row(pack_row(own_cols[q], q, -1), q, ROWS)
    send("tx0", own_cols, left, got_cols.at[0], has_left)
    to_right = copy("tx1", own_cols, got_cols.at[1], right)
    pl.when(greeted_right)(to_right.start)
    started.append((has_right, to_right))
    relay("+", "O1", prev, core, 1)
    relay("-", "O0", nxt, core, 0)
    arrived("SH", held.at[chip * 2 + sib, pl.ds(0, 4)])
    send("+HB", piece(chip, sib, core, "h"), peer(1, 0))
    send("-HB", piece(chip, sib, core, "h"), peer(-1, 0))
    send("+F1", relay("+", "B0", prev, sib, 0), peer(1, 0))
    send("-F1", relay("-", "B1", nxt, sib, 1), peer(-1, 0))
    relay("+", "B1", prev, sib, 1)
    relay("-", "B0", nxt, sib, 0)
    send("+FH", relay("+", "HO", prev, core, "h"), peer(1, 0))
    relay("-", "HO", nxt, core, "h")
    relay("+", "HB", prev, sib, "h")
    send("-FH", relay("-", "HB", nxt, sib, "h"), peer(-1, 0))

    for d, source in (("+", prev), ("-", nxt)):
        for kind, owner, half_piece in (("O0", sib, 0), ("O1", sib, 1), ("B0", core, 0), ("B1", core, 1)):
            arrived("X" + d + kind, piece(source, owner, sib, half_piece))
    gather_rows(pair_prev + pair_next, False)

    def go_right():
        pl.semaphore_wait(leave, 1)
        to_right.start()

    pl.when(needs_leave)(go_right)

    relay("+", "F0", far, core, 0)
    relay("-", "F0", far, core, 1)
    relay("+", "F1", far, sib, 0)
    relay("-", "F1", far, sib, 1)
    relay("+", "FH", far, core, "h")
    relay("-", "FH", far, sib, "h")

    arrived("tx0", got_cols.at[0], has_right)
    arrived("tx1", got_cols.at[1], has_left)
    for q in range(2):
        mine = own_cols[q]
        cols = jnp.where(lane < 64, pltpu.roll(got_cols[1, q], 32, 1), pltpu.roll(got_cols[0, q], 96, 1))
        held[mp, COLS + q] = jnp.where((lane < 32) | (lane >= 96), mine, cols)
    for a, b in peers:
        send("P%d%d" % (a, b), held.at[mp, pl.ds(COLS, 2)], peer(a, b))

    alpha = coupling[mp]
    ratio = tv_weight[mp] / alpha

    def fluxes(m, g, e):
        size_sq = g[0] * g[0] + g[1] * g[1] + g[2] * g[2] + EPS_SQ
        tv = ratio * lax.rsqrt(size_sq)
        a00, a11, a22 = m[1] + m[2] + tv, m[0] + m[2] + tv, m[0] + m[1] + tv
        b00, b11, b22 = m[10] + m[14], m[6] + m[14], m[6] + m[10]
        q = (
            a00 * g[0] - (m[3] * g[1] + m[4] * g[2]),
            a11 * g[1] - (m[3] * g[0] + m[5] * g[2]),
            a22 * g[2] - (m[4] * g[0] + m[5] * g[1]),
        )
        p = (
            (a00 * e[0] + b00 * g[0]) - ((m[3] * e[1] + m[4] * e[2]) + (m[7] * g[1] + m[8] * g[2])),
            (a11 * e[1] + b11 * g[1]) - ((m[3] * e[0] + m[5] * e[2]) + (m[9] * g[0] + m[11] * g[2])),
            (a22 * e[2] + b22 * g[2]) - ((m[4] * e[0] + m[5] * e[1]) + (m[12] * g[0] + m[13] * g[1])),
        )
        return q, p

    def along_z(fz):
        fz = jnp.where(inner_z, fz, 0.0)
        return jnp.where(level == 0, 0.0, pltpu.roll(fz, 1, 0)) - fz

    outs = (gout, hout)

    def put_row(i, both, before_y, keep=None):
        new = []
        for q in range(2):
            fx, fy, fz = both[q]
            if keep is not None:
                fy = fy * keep
            enters = jnp.where(lane == 0, 0.0, pltpu.roll(fx, 1, 1))
            rest = jnp.where(lane == LANES - 1, 0.0, before_y[q] - fy + along_z(fz) - fx)
            outs[q][pl.ds(i - 1, NZ, stride=ROWS), :] = alpha * (enters + rest)
            new.append(fy)
        return tuple(new)

    for name, owner, half_piece in (
        ("X+F0", sib, 0), ("X-F0", sib, 1), ("X+F1", core, 0), ("X-F1", core, 1),
    ):
        arrived(name, piece(far, owner, sib, half_piece))

    def out_body(i, carry):
        acc = row_moments([moms[i, j] for j in range(15)], pair_far, i)
        return put_row(i, fluxes(acc, *row_fields(mp, i)), carry)

    carry = lax.fori_loop(1, ROWS, out_body, (zero, zero), unroll=5)

    for d, source in (("+", prev), ("-", nxt)):
        arrived("X" + d + "HO", piece(source, sib, sib, "h"))
        arrived("X" + d + "HB", piece(source, core, sib, "h"))
    arrived("X+FH", piece(far, sib, sib, "h"))
    arrived("X-FH", piece(far, core, sib, "h"))
    every = pair_own + pair_prev + pair_next + pair_far
    put_row(ROWS, fluxes(row_moments(None, every, ROWS), *row_fields(mp, ROWS)), carry, keep_last)
    keep_first = alpha * jnp.where(has_before, 1.0, 0.0)
    entering = [f[1] * keep_first for f in fluxes(row_moments(None, every, 0), *row_fields(mp, 0))]

    for a, b in peers:
        owner = at_chip(-a) * 2 + (sib if b else core)
        arrived("P%d%d" % (a, b), held.at[owner, pl.ds(COLS, 2)])
    no_x = (lane < 32) & (tx == n_tx - 1)
    no_y = ((lane == ROWS) | (lane == ROWS + 32)) & (ty == n_ty - 1)

    def col_fields(model):
        out = []
        for q in range(2):
            v = held[model, COLS + q]
            dx = jnp.where(no_x, 0.0, pltpu.roll(v, 64, 1) - v)
            dy = jnp.where(no_y, 0.0, pltpu.roll(v, LANES - 1, 1) - v)
            dz = jnp.where(inner_z, pltpu.roll(v, NZ - 1, 0) - v, 0.0)
            out.append((dx, dy, dz))
        return out

    col_moms = None
    for model in range(MODELS):
        g, e = col_fields(model)
        col_moms = add_moments(col_moms, g, e, coupling[model])
    off_x = no_x | ((lane >= 32) & (tx == 0))
    off_y = no_y | ((lane == 0) & (ty == 0))
    for q, f in enumerate(fluxes(col_moms, *col_fields(mp))):
        fx = jnp.where(off_x, 0.0, f[0])
        fy = jnp.where(off_y, 0.0, f[1])
        col_flux[0, q] = alpha * (pltpu.roll(fy, 1, 1) - fy + along_z(f[2]) - fx)
        col_flux[1, q] = alpha * fx
    for q in range(2):
        ends, starts = col_flux[0, q], col_flux[1, q]
        for r in range(ROWS):
            rows = pl.ds(r, NZ, stride=ROWS)
            more = jnp.where(lane == LANES - 1, pltpu.roll(ends, 126 - r, 1), 0.0)
            more = jnp.where(lane == 0, pltpu.roll(starts, 95 - r, 1), more)
            if r == 0:
                more = more + jnp.where(lane == LANES - 1, 0.0, entering[q])
            outs[q][rows, :] = outs[q][rows, :] + more

    for wanted, c in started:
        if wanted is None:
            c.wait_send()
        else:
            pl.when(wanted)(c.wait_send)


def shards(models, direction, coupling, tv_weight):
    flat = (NZ * ROWS, LANES)
    n = len(NAMES)
    out = pl.pallas_call(
        kernel,
        name="fused",
        out_shape=[jax.ShapeDtypeStruct(flat, jnp.float32)] * 2,
        in_specs=[pl.BlockSpec(memory_space=pl.ANY)] * 4,
        out_specs=[pl.BlockSpec(memory_space=pltpu.VMEM)] * 2,
        scratch_shapes=[
            pltpu.VMEM((MODELS, SLABS, NZ, LANES), jnp.float32),
            pltpu.VMEM((2,) + flat, jnp.float32),
            pltpu.VMEM((ROWS + 1, 15, NZ, LANES), jnp.float32),
            pltpu.VMEM((2, NZ, LANES), jnp.float32),
            pltpu.VMEM((2, 2, NZ, LANES), jnp.float32),
            pltpu.VMEM((2, 2, NZ, LANES), jnp.float32),
            pltpu.SMEM((MODELS,), jnp.float32),
            pltpu.SMEM((MODELS,), jnp.float32),
            pltpu.SemaphoreType.DMA((4,)),
            pltpu.SemaphoreType.DMA((n,)),
            pltpu.SemaphoreType.DMA((n,)),
            pltpu.SemaphoreType.REGULAR,
        ],
        compiler_params=pltpu.CompilerParams(
            collective_id=1, has_side_effects=True, vmem_limit_bytes=60 * 2**20
        ),
    )(models.reshape(flat), direction.reshape(flat), coupling, tv_weight)
    return tuple(o.reshape(models.shape) for o in out)


def solution(mesh):
    placed = (P("mp", None, "ty", "tx"), P("mp", None, "ty", "tx"), P(), P())
    return jax.shard_map(
        shards,
        mesh=mesh,
        in_specs=placed,
        out_specs=(P("mp", None, "ty", "tx"), P("mp", None, "ty", "tx")),
        check_vma=False,
    )
```

time: 38.6 us -> 31.7 us (0.82)
  Pallas kernels: 35.6 us -> 28.6 us
    pallas_call x1, Pallas kernels: 35.6 us -> 28.6 us  [shards(): pl.pallas_call(kernel, name='fused', out_shape=[jax.ShapeDtypeStruct(flat...]
where the time goes in v2:
time: 31.7 us; the launch traced here: 31.5 us
  Pallas kernels  28.6 us (90%)
  local copies, waits for them, and re-layouts  2.26 us (7%)
  between operations  0.65 us (2%)
    pallas_call x1, Pallas kernels, shards(): pl.pallas_call(kernel, name='fused', out_shape=[jax.ShapeDtypeStruct(flat...  28.6 us
    unnamed x4, local copies, waits for them, and re-layouts  2.26 us

profile of v2, /device:TPU:1, one launch (start us, length us, event | category | flops | bytes accessed | tf_op | source)
XLA Modules:
  0.0 31.5 jit_solution(2750572238302555250)
XLA Ops:
  0.6 28.6 %fused.1 = (f32[256,128]{1,0:T(8,128)}, f32[256,128]{1,0:T(8,128)}) custom-call(f32[256,128]{1,0:T(8,128)} %bitcast.4, f32[256,128]{1,0:T(8,128)} %bitcast.5, f32[8]{0:T(128)} %coupling_hbm.1, f32[8]{0:T(128)} %tv_hbm.1), custom_call_target="tpu_custom_call" | custom-call | tf_op jit(solution)/shard_map/fused/pallas_call | solution.py:369
  29.3 0.0 copy-start
  29.3 1.6 %copy.8 = f32[1,16,16,128]{3,2,1,0:T(8,128)} copy(f32[1,16,16,128]{3,2,1,0:T(8,128)} %bitcast.7) | data formatting | bytes 262144
  30.9 0.0 copy-done
  30.9 0.7 %copy.9 = f32[1,16,16,128]{3,2,1,0:T(8,128)} copy(f32[1,16,16,128]{3,2,1,0:T(8,128)S(1)} %bitcast.6) | data formatting | bytes 262144
Async XLA Ops:
  29.3 1.6 %copy-start = (f32[256,128]{1,0:T(8,128)S(1)}, f32[256,128]{1,0:T(8,128)}, u32[]{:S(2)}) copy-start(f32[256,128]{1,0:T(8,128)} %get-tuple-element.5) | copy-start | bytes 393220

commit v3 on v2

--- a/solution.py
+++ b/solution.py
@@ -17,11 +17,11 @@
 SLABS = 38
 COLS = 36
 
-RING = ("O0", "O1", "B0", "B1", "HO", "HB", "F0", "F1", "FH")
+RING = ("O0", "O1", "O2", "O3", "H", "F0", "F1")
 NAMES = (
-    ["ty0", "ty1", "tx0", "tx1", "S1", "S0", "SH"]
-    + [d + k for d in "+-" for k in RING]
-    + ["X" + d + k for d in "+-" for k in RING]
+    ["ty0", "ty1", "tx0", "tx1", "S", "SH"]
+    + [d + k for d in "+-" for k in RING] + ["2H"]
+    + ["X" + d + k for d in "+-" for k in RING] + ["X2H"]
     + ["P%d%d" % (a, b) for a in range(CHIPS) for b in range(2) if a + b > 0]
 )
 INDEX = {name: i for i, name in enumerate(NAMES)}
@@ -97,13 +97,9 @@
         else:
             pl.when(wanted)(wait)
 
-    def piece(owner_chip, owner_core, half, kind):
-        model = owner_chip * 2 + owner_core
-        if kind == "h":
-            return held.at[model, pl.ds(2 - 2 * half, 2)]
-        if kind == "all":
-            return held.at[model, pl.ds(4 + 16 * half, 16)]
-        return held.at[model, pl.ds(4 + 16 * half + 8 * kind, 8)]
+    def piece(model, part):
+        first, n = {"H": (0, 4), "all": (4, 32)}.get(part) or (4 + 8 * part, 8)
+        return held.at[model, pl.ds(first, n)]
 
     def pack_row(cols, q, r):
         v = held[mp, 2 * ((r + 2) % 18) + q]
@@ -137,23 +133,17 @@
 
     send("ty0", held.at[mp, pl.ds(4, 2)], before, rim_after, has_before)
     send("ty1", held.at[mp, pl.ds(34, 2)], after, rim_before, has_after)
-    send("S1", piece(chip, core, sib, "all"), peer(0, 1))
-    send("+O0", piece(chip, core, core, 0), peer(1, 0))
-    send("-O1", piece(chip, core, core, 1), peer(-1, 0))
-    send("+O1", piece(chip, core, core, 1), peer(1, 0))
-    send("-O0", piece(chip, core, core, 0), peer(-1, 0))
-    send("S0", piece(chip, core, core, "all"), peer(0, 1))
+    for up, down in ((0, 2), (1, 3), (2, 0), (3, 1)):
+        send("+O%d" % up, piece(mp, up), peer(1, 0))
+        send("-O%d" % down, piece(mp, down), peer(-1, 0))
+        if up == 1:
+            send("S", piece(mp, "all"), peer(0, 1))
 
     def give_leave():
         pl.semaphore_signal(leave, inc=1, device_id=left, device_id_type=MESH)
 
     pl.when(gives_leave)(give_leave)
-    arrived("S1", piece(chip, sib, core, "all"))
-    send("+B0", piece(chip, sib, core, 0), peer(1, 0))
-    send("-B1", piece(chip, sib, core, 1), peer(-1, 0))
-    send("+B1", piece(chip, sib, core, 1), peer(1, 0))
-    send("-B0", piece(chip, sib, core, 0), peer(-1, 0))
-    arrived("S0", piece(chip, sib, sib, "all"))
+    arrived("S", piece(chip * 2 + sib, "all"))
 
     def differences(f, f_next, keep_y=None):
         dx = pltpu.roll(f, LANES - 1, 1) - f
@@ -196,61 +186,56 @@
         lax.fori_loop(1, ROWS, body, 0, unroll=5)
 
     prev, nxt, far = at_chip(-1), at_chip(1), at_chip(2)
-    pair_own, pair_prev, pair_next, pair_far = ([c * 2, c * 2 + 1] for c in (chip, prev, nxt, far))
-
-    def relay(d, kind, source, owner_core, half_piece):
-        ref = piece(source, owner_core, core, half_piece)
+    pair_own, pair_far = [chip * 2, chip * 2 + 1], [far * 2, far * 2 + 1]
+
+    def relay(d, kind, source, part):
+        ref = piece(source * 2 + core, part)
         arrived(d + kind, ref)
         send("X" + d + kind, ref, peer(0, 1))
-        return ref
+
+    def onward(d, kind, source, part):
+        send(d + kind, piece(source * 2 + core, part), peer(1 if d == "+" else -1, 0))
+
+    def from_sibling(d, kind, source, part):
+        arrived("X" + d + kind, piece(source * 2 + sib, part))
 
     gather_rows(pair_own, True)
 
-    send("+F0", relay("+", "O0", prev, core, 0), peer(1, 0))
-    send("-F0", relay("-", "O1", nxt, core, 1), peer(-1, 0))
+    relay("+", "O0", prev, 0)
+    onward("+", "F0", prev, 0)
+    relay("-", "O2", nxt, 2)
+    onward("-", "F0", nxt, 2)
     arrived("ty0", rim_after, has_after)
     arrived("ty1", rim_before, has_before)
-    send("SH", held.at[mp, pl.ds(0, 4)], peer(0, 1))
-    send("+HO", piece(chip, core, core, "h"), peer(1, 0))
-    send("-HO", piece(chip, core, core, "h"), peer(-1, 0))
+    send("+H", piece(mp, "H"), peer(1, 0))
+    send("-H", piece(mp, "H"), peer(-1, 0))
+    send("2H", piece(mp, "H"), peer(2, 0))
+    send("SH", piece(mp, "H"), peer(0, 1))
     for q in range(2):
         own_cols[q] = pack_row(pack_row(own_cols[q], q, -1), q, ROWS)
     send("tx0", own_cols, left, got_cols.at[0], has_left)
     to_right = copy("tx1", own_cols, got_cols.at[1], right)
     pl.when(greeted_right)(to_right.start)
     started.append((has_right, to_right))
-    relay("+", "O1", prev, core, 1)
-    relay("-", "O0", nxt, core, 0)
-    arrived("SH", held.at[chip * 2 + sib, pl.ds(0, 4)])
-    send("+HB", piece(chip, sib, core, "h"), peer(1, 0))
-    send("-HB", piece(chip, sib, core, "h"), peer(-1, 0))
-    send("+F1", relay("+", "B0", prev, sib, 0), peer(1, 0))
-    send("-F1", relay("-", "B1", nxt, sib, 1), peer(-1, 0))
-    relay("+", "B1", prev, sib, 1)
-    relay("-", "B0", nxt, sib, 0)
-    send("+FH", relay("+", "HO", prev, core, "h"), peer(1, 0))
-    relay("-", "HO", nxt, core, "h")
-    relay("+", "HB", prev, sib, "h")
-    send("-FH", relay("-", "HB", nxt, sib, "h"), peer(-1, 0))
-
-    for d, source in (("+", prev), ("-", nxt)):
-        for kind, owner, half_piece in (("O0", sib, 0), ("O1", sib, 1), ("B0", core, 0), ("B1", core, 1)):
-            arrived("X" + d + kind, piece(source, owner, sib, half_piece))
-    gather_rows(pair_prev + pair_next, False)
-
+    relay("+", "O1", prev, 1)
+    onward("+", "F1", prev, 1)
+    relay("-", "O3", nxt, 3)
+    onward("-", "F1", nxt, 3)
+    relay("+", "O2", prev, 2)
+    relay("-", "O0", nxt, 0)
+    relay("+", "O3", prev, 3)
+    relay("-", "O1", nxt, 1)
+    gather_rows([prev * 2 + core, nxt * 2 + core], False)
+    relay("+", "H", prev, "H")
+    relay("-", "H", nxt, "H")
+    relay("2", "H", far, "H")
+    relay("+", "F0", far, 0)
+    relay("-", "F0", far, 2)
     def go_right():
         pl.semaphore_wait(leave, 1)
         to_right.start()
 
     pl.when(needs_leave)(go_right)
-
-    relay("+", "F0", far, core, 0)
-    relay("-", "F0", far, core, 1)
-    relay("+", "F1", far, sib, 0)
-    relay("-", "F1", far, sib, 1)
-    relay("+", "FH", far, core, "h")
-    relay("-", "FH", far, sib, "h")
-
     arrived("tx0", got_cols.at[0], has_right)
     arrived("tx1", got_cols.at[1], has_left)
     for q in range(2):
@@ -259,6 +244,13 @@
         held[mp, COLS + q] = jnp.where((lane < 32) | (lane >= 96), mine, cols)
     for a, b in peers:
         send("P%d%d" % (a, b), held.at[mp, pl.ds(COLS, 2)], peer(a, b))
+
+    relay("+", "F1", far, 1)
+    relay("-", "F1", far, 3)
+    for k in range(4):
+        from_sibling("+", "O%d" % k, prev, k)
+        from_sibling("-", "O%d" % k, nxt, k)
+    gather_rows([prev * 2 + sib, nxt * 2 + sib], False)
 
     alpha = coupling[mp]
     ratio = tv_weight[mp] / alpha
@@ -298,10 +290,9 @@
             new.append(fy)
         return tuple(new)
 
-    for name, owner, half_piece in (
-        ("X+F0", sib, 0), ("X-F0", sib, 1), ("X+F1", core, 0), ("X-F1", core, 1),
-    ):
-        arrived(name, piece(far, owner, sib, half_piece))
+    for d, first in (("+", 0), ("-", 2)):
+        from_sibling(d, "F0", far, first)
+        from_sibling(d, "F1", far, first + 1)
 
     def out_body(i, carry):
         acc = row_moments([moms[i, j] for j in range(15)], pair_far, i)
@@ -309,12 +300,11 @@
 
     carry = lax.fori_loop(1, ROWS, out_body, (zero, zero), unroll=5)
 
-    for d, source in (("+", prev), ("-", nxt)):
-        arrived("X" + d + "HO", piece(source, sib, sib, "h"))
-        arrived("X" + d + "HB", piece(source, core, sib, "h"))
-    arrived("X+FH", piece(far, sib, sib, "h"))
-    arrived("X-FH", piece(far, core, sib, "h"))
-    every = pair_own + pair_prev + pair_next + pair_far
+    arrived("SH", piece(chip * 2 + sib, "H"))
+    from_sibling("+", "H", prev, "H")
+    from_sibling("-", "H", nxt, "H")
+    from_sibling("2", "H", far, "H")
+    every = range(MODELS)
     put_row(ROWS, fluxes(row_moments(None, every, ROWS), *row_fields(mp, ROWS)), carry, keep_last)
     keep_first = alpha * jnp.where(has_before, 1.0, 0.0)
     entering = [f[1] * keep_first for f in fluxes(row_moments(None, every, 0), *row_fields(mp, 0))]
@@ -369,7 +359,7 @@
     out = pl.pallas_call(
         kernel,
         name="fused",
-        out_shape=[jax.ShapeDtypeStruct(flat, jnp.float32)] * 2,
+        out_shape=[pltpu.VMEM(flat, jnp.float32)] * 2,
         in_specs=[pl.BlockSpec(memory_space=pl.ANY)] * 4,
         out_specs=[pl.BlockSpec(memory_space=pltpu.VMEM)] * 2,
         scratch_shapes=[

time: 31.7 us -> 27.9 us (0.88)
  the two profiles are of different devices: /device:TPU:1 before, /device:TPU:7 now
where the time goes in v3:
time: 27.9 us; the launch traced here: 27.7 us
  Pallas kernels  25.8 us (92%)
  local copies, waits for them, and re-layouts  1.31 us (5%)
  between operations  0.64 us (2%)
    pallas_call x1, Pallas kernels, shards(): pl.pallas_call(kernel, name='fused', out_shape=[pltpu.VMEM(flat, jnp.floa...  25.8 us
    unnamed x2, local copies, waits for them, and re-layouts  1.31 us

profile of v3, /device:TPU:7, one launch (start us, length us, event | category | flops | bytes accessed | tf_op | source)
XLA Modules:
  0.0 27.7 jit_solution(2104692473718807226)
XLA Ops:
  0.6 25.8 %fused.1 = (f32[256,128]{1,0:T(8,128)S(1)}, f32[256,128]{1,0:T(8,128)S(1)}) custom-call(f32[256,128]{1,0:T(8,128)} %bitcast.6, f32[256,128]{1,0:T(8,128)} %bitcast.7, f32[8]{0:T(128)} %coupling_hbm.1, f32[8]{0:T(128)} %tv_hbm.1), custom_call_target="tpu_custom_call" | custom-call | tf_op jit(solution)/shard_map/fused/pallas_call | solution.py:359
  26.4 0.7 %copy.8 = f32[1,16,16,128]{3,2,1,0:T(8,128)} copy(f32[1,16,16,128]{3,2,1,0:T(8,128)S(1)} %bitcast.5) | data formatting | bytes 262144
  27.1 0.7 %copy.9 = f32[1,16,16,128]{3,2,1,0:T(8,128)} copy(f32[1,16,16,128]{3,2,1,0:T(8,128)S(1)} %bitcast.4) | data formatting | bytes 262144

commit v4 on v3

--- a/solution.py
+++ b/solution.py
@@ -28,7 +28,7 @@
 
 
 def kernel(
-    x_hbm, d_hbm, coupling_hbm, tv_hbm, gout, hout,
+    x_hbm, d_hbm, coupling_hbm, tv_hbm, outs,
     held, tile, moms, own_cols, got_cols, col_flux, coupling, tv_weight, in_sem, send_sem, recv_sem, leave,
 ):
     mp, tx, ty = (lax.axis_index(a) for a in ("mp", "tx", "ty"))
@@ -48,7 +48,7 @@
     greets_left, greeted_right = tx == n_tx - 1, tx == n_tx - 2
     gives_leave = has_left & jnp.logical_not(greets_left)
     needs_leave = has_right & jnp.logical_not(greeted_right)
-    peers = [(a, b) for a in range(CHIPS) for b in range(2) if a + b > 0]
+    peers = [(2, 0), (2, 1), (1, 0), (3, 0), (1, 1), (3, 1), (0, 1)]
 
     barrier = pltpu.get_barrier_semaphore()
 
@@ -276,8 +276,6 @@
         fz = jnp.where(inner_z, fz, 0.0)
         return jnp.where(level == 0, 0.0, pltpu.roll(fz, 1, 0)) - fz
 
-    outs = (gout, hout)
-
     def put_row(i, both, before_y, keep=None):
         new = []
         for q in range(2):
@@ -286,7 +284,7 @@
                 fy = fy * keep
             enters = jnp.where(lane == 0, 0.0, pltpu.roll(fx, 1, 1))
             rest = jnp.where(lane == LANES - 1, 0.0, before_y[q] - fy + along_z(fz) - fx)
-            outs[q][pl.ds(i - 1, NZ, stride=ROWS), :] = alpha * (enters + rest)
+            outs[q, pl.ds(i - 1, NZ, stride=ROWS), :] = alpha * (enters + rest)
             new.append(fy)
         return tuple(new)
 
@@ -309,6 +307,11 @@
     keep_first = alpha * jnp.where(has_before, 1.0, 0.0)
     entering = [f[1] * keep_first for f in fluxes(row_moments(None, every, 0), *row_fields(mp, 0))]
 
+    for wanted, c in started:
+        if wanted is None:
+            c.wait_send()
+        else:
+            pl.when(wanted)(c.wait_send)
     for a, b in peers:
         owner = at_chip(-a) * 2 + (sib if b else core)
         arrived("P%d%d" % (a, b), held.at[owner, pl.ds(COLS, 2)])
@@ -344,13 +347,7 @@
             more = jnp.where(lane == 0, pltpu.roll(starts, 95 - r, 1), more)
             if r == 0:
                 more = more + jnp.where(lane == LANES - 1, 0.0, entering[q])
-            outs[q][rows, :] = outs[q][rows, :] + more
-
-    for wanted, c in started:
-        if wanted is None:
-            c.wait_send()
-        else:
-            pl.when(wanted)(c.wait_send)
+            outs[q, rows, :] = outs[q, rows, :] + more
 
 
 def shards(models, direction, coupling, tv_weight):
@@ -359,9 +356,9 @@
     out = pl.pallas_call(
         kernel,
         name="fused",
-        out_shape=[pltpu.VMEM(flat, jnp.float32)] * 2,
+        out_shape=pltpu.VMEM((2,) + flat, jnp.float32),
         in_specs=[pl.BlockSpec(memory_space=pl.ANY)] * 4,
-        out_specs=[pl.BlockSpec(memory_space=pltpu.VMEM)] * 2,
+        out_specs=pl.BlockSpec(memory_space=pltpu.VMEM),
         scratch_shapes=[
             pltpu.VMEM((MODELS, SLABS, NZ, LANES), jnp.float32),
             pltpu.VMEM((2,) + flat, jnp.float32),
@@ -380,7 +377,7 @@
             collective_id=1, has_side_effects=True, vmem_limit_bytes=60 * 2**20
         ),
     )(models.reshape(flat), direction.reshape(flat), coupling, tv_weight)
-    return tuple(o.reshape(models.shape) for o in out)
+    return tuple(out[q].reshape(models.shape) for q in range(2))
 
 
 def solution(mesh):

time: 27.9 us -> 26.9 us (0.964)
  the two profiles are of different devices: /device:TPU:7 before, /device:TPU:1 now
where the time goes in v4:
time: 26.9 us; the launch traced here: 26.5 us
  Pallas kernels  25.1 us (93%)
  local copies, waits for them, and re-layouts  0.72 us (3%)
  between operations  0.64 us (2%)
    pallas_call x1, Pallas kernels, shards(): pl.pallas_call(kernel, name='fused', out_shape=pltpu.VMEM((2,) + flat, jn...  25.1 us
    slice x1, local copies, waits for them, and re-layouts, shards(): return tuple((out[q].reshape(models.shape) for q in range(2)))  0.72 us

profile of v4, /device:TPU:1, one launch (start us, length us, event | category | flops | bytes accessed | tf_op | source)
XLA Modules:
  0.0 26.5 jit_solution(42588549047703899)
XLA Ops:
  0.6 25.1 %fused.1 = f32[2,256,128]{2,1,0:T(8,128)S(1)} custom-call(f32[256,128]{1,0:T(8,128)} %bitcast.4, f32[256,128]{1,0:T(8,128)} %bitcast.5, f32[8]{0:T(128)} %coupling_hbm.1, f32[8]{0:T(128)} %tv_hbm.1), custom_call_target="tpu_custom_call" | custom-call | tf_op jit(solution)/shard_map/fused/pallas_call | solution.py:356
  25.7 0.7 %fusion = (f32[1,256,128]{2,1,0:T(8,128)}, f32[1,256,128]{2,1,0:T(8,128)}) fusion(f32[2,256,128]{2,1,0:T(8,128)S(1)} %fused.1), kind=kLoop, calls=%fused_computation | loop fusion | bytes 524288 | tf_op jit(solution)/shard_map/slice | solution.py:380

commit v5 on v4

--- a/solution.py
+++ b/solution.py
@@ -143,8 +143,6 @@
         pl.semaphore_signal(leave, inc=1, device_id=left, device_id_type=MESH)
 
     pl.when(gives_leave)(give_leave)
-    arrived("S", piece(chip * 2 + sib, "all"))
-
     def differences(f, f_next, keep_y=None):
         dx = pltpu.roll(f, LANES - 1, 1) - f
         dy = f_next - f
@@ -199,28 +197,28 @@
     def from_sibling(d, kind, source, part):
         arrived("X" + d + kind, piece(source * 2 + sib, part))
 
-    gather_rows(pair_own, True)
-
-    relay("+", "O0", prev, 0)
-    onward("+", "F0", prev, 0)
-    relay("-", "O2", nxt, 2)
-    onward("-", "F0", nxt, 2)
     arrived("ty0", rim_after, has_after)
     arrived("ty1", rim_before, has_before)
-    send("+H", piece(mp, "H"), peer(1, 0))
-    send("-H", piece(mp, "H"), peer(-1, 0))
-    send("2H", piece(mp, "H"), peer(2, 0))
-    send("SH", piece(mp, "H"), peer(0, 1))
     for q in range(2):
         own_cols[q] = pack_row(pack_row(own_cols[q], q, -1), q, ROWS)
     send("tx0", own_cols, left, got_cols.at[0], has_left)
     to_right = copy("tx1", own_cols, got_cols.at[1], right)
     pl.when(greeted_right)(to_right.start)
     started.append((has_right, to_right))
+    relay("+", "O0", prev, 0)
+    onward("+", "F0", prev, 0)
+    relay("-", "O2", nxt, 2)
+    onward("-", "F0", nxt, 2)
+    send("+H", piece(mp, "H"), peer(1, 0))
+    send("-H", piece(mp, "H"), peer(-1, 0))
+    send("2H", piece(mp, "H"), peer(2, 0))
+    send("SH", piece(mp, "H"), peer(0, 1))
     relay("+", "O1", prev, 1)
     onward("+", "F1", prev, 1)
     relay("-", "O3", nxt, 3)
     onward("-", "F1", nxt, 3)
+    arrived("S", piece(chip * 2 + sib, "all"))
+    gather_rows(pair_own, True)
     relay("+", "O2", prev, 2)
     relay("-", "O0", nxt, 0)
     relay("+", "O3", prev, 3)

time: 26.9 us -> 26.6 us (0.989); the launches traced: 26.5 us -> 26.5 us
  no operation moved by 1% of the time
where the time goes in v5:
time: 26.6 us; the launch traced here: 26.5 us
  Pallas kernels  25.1 us (94%)
  local copies, waits for them, and re-layouts  0.72 us (3%)
  between operations  0.64 us (2%)
    pallas_call x1, Pallas kernels, shards(): pl.pallas_call(kernel, name='fused', out_shape=pltpu.VMEM((2,) + flat, jn...  25.1 us
    slice x1, local copies, waits for them, and re-layouts, shards(): return tuple((out[q].reshape(models.shape) for q in range(2)))  0.72 us

profile of v5, /device:TPU:1, one launch (start us, length us, event | category | flops | bytes accessed | tf_op | source)
XLA Modules:
  0.0 26.5 jit_solution(14011356712698232198)
XLA Ops:
  0.6 25.1 %fused.1 = f32[2,256,128]{2,1,0:T(8,128)S(1)} custom-call(f32[256,128]{1,0:T(8,128)} %bitcast.4, f32[256,128]{1,0:T(8,128)} %bitcast.5, f32[8]{0:T(128)} %coupling_hbm.1, f32[8]{0:T(128)} %tv_hbm.1), custom_call_target="tpu_custom_call" | custom-call | tf_op jit(solution)/shard_map/fused/pallas_call | solution.py:354
  25.7 0.7 %fusion = (f32[1,256,128]{2,1,0:T(8,128)}, f32[1,256,128]{2,1,0:T(8,128)}) fusion(f32[2,256,128]{2,1,0:T(8,128)S(1)} %fused.1), kind=kLoop, calls=%fused_computation | loop fusion | bytes 524288 | tf_op jit(solution)/shard_map/slice | solution.py:378

commit v6 on v5

--- a/solution.py
+++ b/solution.py
@@ -209,14 +209,14 @@
     onward("+", "F0", prev, 0)
     relay("-", "O2", nxt, 2)
     onward("-", "F0", nxt, 2)
+    relay("+", "O1", prev, 1)
+    onward("+", "F1", prev, 1)
+    relay("-", "O3", nxt, 3)
+    onward("-", "F1", nxt, 3)
     send("+H", piece(mp, "H"), peer(1, 0))
     send("-H", piece(mp, "H"), peer(-1, 0))
     send("2H", piece(mp, "H"), peer(2, 0))
     send("SH", piece(mp, "H"), peer(0, 1))
-    relay("+", "O1", prev, 1)
-    onward("+", "F1", prev, 1)
-    relay("-", "O3", nxt, 3)
-    onward("-", "F1", nxt, 3)
     arrived("S", piece(chip * 2 + sib, "all"))
     gather_rows(pair_own, True)
     relay("+", "O2", prev, 2)
@@ -224,11 +224,9 @@
     relay("+", "O3", prev, 3)
     relay("-", "O1", nxt, 1)
     gather_rows([prev * 2 + core, nxt * 2 + core], False)
-    relay("+", "H", prev, "H")
-    relay("-", "H", nxt, "H")
-    relay("2", "H", far, "H")
     relay("+", "F0", far, 0)
     relay("-", "F0", far, 2)
+
     def go_right():
         pl.semaphore_wait(leave, 1)
         to_right.start()
@@ -245,6 +243,9 @@
 
     relay("+", "F1", far, 1)
     relay("-", "F1", far, 3)
+    relay("+", "H", prev, "H")
+    relay("-", "H", nxt, "H")
+    relay("2", "H", far, "H")
     for k in range(4):
         from_sibling("+", "O%d" % k, prev, k)
         from_sibling("-", "O%d" % k, nxt, k)

time: 26.6 us -> 26.2 us (0.985)
  Pallas kernels: 25.1 us -> 24.7 us
    pallas_call x1, Pallas kernels: 25.1 us -> 24.7 us  [shards(): pl.pallas_call(kernel, name='fused', out_shape=pltpu.VMEM((2,) + flat, jn...]
where the time goes in v6:
time: 26.2 us; the launch traced here: 26.1 us
  Pallas kernels  24.7 us (94%)
  local copies, waits for them, and re-layouts  0.72 us (3%)
  between operations  0.64 us (2%)
    pallas_call x1, Pallas kernels, shards(): pl.pallas_call(kernel, name='fused', out_shape=pltpu.VMEM((2,) + flat, jn...  24.7 us
    slice x1, local copies, waits for them, and re-layouts, shards(): return tuple((out[q].reshape(models.shape) for q in range(2)))  0.72 us

profile of v6, /device:TPU:1, one launch (start us, length us, event | category | flops | bytes accessed | tf_op | source)
XLA Modules:
  0.0 26.1 jit_solution(5206944031860616453)
XLA Ops:
  0.6 24.7 %fused.1 = f32[2,256,128]{2,1,0:T(8,128)S(1)} custom-call(f32[256,128]{1,0:T(8,128)} %bitcast.4, f32[256,128]{1,0:T(8,128)} %bitcast.5, f32[8]{0:T(128)} %coupling_hbm.1, f32[8]{0:T(128)} %tv_hbm.1), custom_call_target="tpu_custom_call" | custom-call | tf_op jit(solution)/shard_map/fused/pallas_call | solution.py:355
  25.4 0.7 %fusion = (f32[1,256,128]{2,1,0:T(8,128)}, f32[1,256,128]{2,1,0:T(8,128)}) fusion(f32[2,256,128]{2,1,0:T(8,128)S(1)} %fused.1), kind=kLoop, calls=%fused_computation | loop fusion | bytes 524288 | tf_op jit(solution)/shard_map/slice | solution.py:379

commit v7 on v6

--- a/solution.py
+++ b/solution.py
@@ -136,7 +136,7 @@
     for up, down in ((0, 2), (1, 3), (2, 0), (3, 1)):
         send("+O%d" % up, piece(mp, up), peer(1, 0))
         send("-O%d" % down, piece(mp, down), peer(-1, 0))
-        if up == 1:
+        if up == 3:
             send("S", piece(mp, "all"), peer(0, 1))
 
     def give_leave():

time: 26.2 us -> 26.2 us (level)
  no operation moved by 1% of the time
where the time goes in v7:
time: 26.2 us; the launch traced here: 26.1 us
  Pallas kernels  24.7 us (94%)
  local copies, waits for them, and re-layouts  0.72 us (3%)
  between operations  0.64 us (2%)
    pallas_call x1, Pallas kernels, shards(): pl.pallas_call(kernel, name='fused', out_shape=pltpu.VMEM((2,) + flat, jn...  24.7 us
    slice x1, local copies, waits for them, and re-layouts, shards(): return tuple((out[q].reshape(models.shape) for q in range(2)))  0.72 us

profile of v7, /device:TPU:1, one launch (start us, length us, event | category | flops | bytes accessed | tf_op | source)
XLA Modules:
  0.0 26.1 jit_solution(8894821855344217809)
XLA Ops:
  0.6 24.7 %fused.1 = f32[2,256,128]{2,1,0:T(8,128)S(1)} custom-call(f32[256,128]{1,0:T(8,128)} %bitcast.4, f32[256,128]{1,0:T(8,128)} %bitcast.5, f32[8]{0:T(128)} %coupling_hbm.1, f32[8]{0:T(128)} %tv_hbm.1), custom_call_target="tpu_custom_call" | custom-call | tf_op jit(solution)/shard_map/fused/pallas_call | solution.py:355
  25.4 0.7 %fusion = (f32[1,256,128]{2,1,0:T(8,128)}, f32[1,256,128]{2,1,0:T(8,128)}) fusion(f32[2,256,128]{2,1,0:T(8,128)S(1)} %fused.1), kind=kLoop, calls=%fused_computation | loop fusion | bytes 524288 | tf_op jit(solution)/shard_map/slice | solution.py:379

commit v8 on v7

--- a/solution.py
+++ b/solution.py
@@ -186,9 +186,11 @@
     prev, nxt, far = at_chip(-1), at_chip(1), at_chip(2)
     pair_own, pair_far = [chip * 2, chip * 2 + 1], [far * 2, far * 2 + 1]
 
-    def relay(d, kind, source, part):
+    def relay(d, kind, source, part, on=None):
         ref = piece(source * 2 + core, part)
         arrived(d + kind, ref)
+        if on is not None:
+            onward(d, on, source, part)
         send("X" + d + kind, ref, peer(0, 1))
 
     def onward(d, kind, source, part):
@@ -205,14 +207,10 @@
     to_right = copy("tx1", own_cols, got_cols.at[1], right)
     pl.when(greeted_right)(to_right.start)
     started.append((has_right, to_right))
-    relay("+", "O0", prev, 0)
-    onward("+", "F0", prev, 0)
-    relay("-", "O2", nxt, 2)
-    onward("-", "F0", nxt, 2)
-    relay("+", "O1", prev, 1)
-    onward("+", "F1", prev, 1)
-    relay("-", "O3", nxt, 3)
-    onward("-", "F1", nxt, 3)
+    relay("+", "O0", prev, 0, "F0")
+    relay("-", "O2", nxt, 2, "F0")
+    relay("+", "O1", prev, 1, "F1")
+    relay("-", "O3", nxt, 3, "F1")
     send("+H", piece(mp, "H"), peer(1, 0))
     send("-H", piece(mp, "H"), peer(-1, 0))
     send("2H", piece(mp, "H"), peer(2, 0))

time: 26.2 us -> 26.2 us (level)
  no operation moved by 1% of the time
where the time goes in v8:
time: 26.2 us; the launch traced here: 26.1 us
  Pallas kernels  24.7 us (94%)
  local copies, waits for them, and re-layouts  0.72 us (3%)
  between operations  0.64 us (2%)
    pallas_call x1, Pallas kernels, shards(): pl.pallas_call(kernel, name='fused', out_shape=pltpu.VMEM((2,) + flat, jn...  24.7 us
    slice x1, local copies, waits for them, and re-layouts, shards(): return tuple((out[q].reshape(models.shape) for q in range(2)))  0.72 us

profile of v8, /device:TPU:1, one launch (start us, length us, event | category | flops | bytes accessed | tf_op | source)
XLA Modules:
  0.0 26.1 jit_solution(7929597516899025677)
XLA Ops:
  0.6 24.7 %fused.1 = f32[2,256,128]{2,1,0:T(8,128)S(1)} custom-call(f32[256,128]{1,0:T(8,128)} %bitcast.4, f32[256,128]{1,0:T(8,128)} %bitcast.5, f32[8]{0:T(128)} %coupling_hbm.1, f32[8]{0:T(128)} %tv_hbm.1), custom_call_target="tpu_custom_call" | custom-call | tf_op jit(solution)/shard_map/fused/pallas_call | solution.py:353
  25.4 0.7 %fusion = (f32[1,256,128]{2,1,0:T(8,128)}, f32[1,256,128]{2,1,0:T(8,128)}) fusion(f32[2,256,128]{2,1,0:T(8,128)S(1)} %fused.1), kind=kLoop, calls=%fused_computation | loop fusion | bytes 524288 | tf_op jit(solution)/shard_map/slice | solution.py:377

commit v9 on v7

--- a/solution.py
+++ b/solution.py
@@ -213,9 +213,9 @@
     onward("+", "F1", prev, 1)
     relay("-", "O3", nxt, 3)
     onward("-", "F1", nxt, 3)
+    send("2H", piece(mp, "H"), peer(2, 0))
     send("+H", piece(mp, "H"), peer(1, 0))
     send("-H", piece(mp, "H"), peer(-1, 0))
-    send("2H", piece(mp, "H"), peer(2, 0))
     send("SH", piece(mp, "H"), peer(0, 1))
     arrived("S", piece(chip * 2 + sib, "all"))
     gather_rows(pair_own, True)

time: 26.2 us -> 26.3 us (level)
  no operation moved by 1% of the time
where the time goes in v9:
time: 26.3 us; the launch traced here: 26.1 us
  Pallas kernels  24.8 us (94%)
  local copies, waits for them, and re-layouts  0.72 us (3%)
  between operations  0.64 us (2%)
    pallas_call x1, Pallas kernels, shards(): pl.pallas_call(kernel, name='fused', out_shape=pltpu.VMEM((2,) + flat, jn...  24.8 us
    slice x1, local copies, waits for them, and re-layouts, shards(): return tuple((out[q].reshape(models.shape) for q in range(2)))  0.72 us

profile of v9, /device:TPU:1, one launch (start us, length us, event | category | flops | bytes accessed | tf_op | source)
XLA Modules:
  0.0 26.1 jit_solution(11407897554829149711)
XLA Ops:
  0.6 24.8 %fused.1 = f32[2,256,128]{2,1,0:T(8,128)S(1)} custom-call(f32[256,128]{1,0:T(8,128)} %bitcast.4, f32[256,128]{1,0:T(8,128)} %bitcast.5, f32[8]{0:T(128)} %coupling_hbm.1, f32[8]{0:T(128)} %tv_hbm.1), custom_call_target="tpu_custom_call" | custom-call | tf_op jit(solution)/shard_map/fused/pallas_call | solution.py:355
  25.4 0.7 %fusion = (f32[1,256,128]{2,1,0:T(8,128)}, f32[1,256,128]{2,1,0:T(8,128)}) fusion(f32[2,256,128]{2,1,0:T(8,128)S(1)} %fused.1), kind=kLoop, calls=%fused_computation | loop fusion | bytes 524288 | tf_op jit(solution)/shard_map/slice | solution.py:379
